TPU v7x, 32 devices: a whole 2x2x4 slice. The times are simulated.
32 devices in a mesh: loop: 16 (over z, y, core), lane: 2 (over x).
Axes of the slice: x: 2, y: 2, z: 4, core: 2. Of those that a mesh axis runs over, the one named last changes fastest.
Arguments:
- orbitals: bfloat16 [8192, 512], P('loop', 'lane'), may hold values from -6 to 6
- coulomb: bfloat16 [16, 2, 2, 512, 512], P('loop', 'lane'), may hold values from -0.01171875 to 0.01171875
- table: int32 [2, 2], P('lane'), may hold values from 0 to 8, as said below
Outputs:
- exchanged: bfloat16 [8192, 512], P('loop', 'lane')
Inputs may be any that keep to these rules, and one draw needn't show every extreme that they name: `table`: the entries are distinct distances; 0 and 8 are always among them.
All inputs are finite; a program needn't handle non-finite values.
Results may differ from a plain program's by a relative error of at most 0.0053.
Values may be sent and summed in bfloat16 or wider, within the bound.
A program may use at most 64 MiB of HBM per device.

v0:
```python
import jax
import jax.numpy as jnp
from jax import lax
from jax.sharding import PartitionSpec as P


def from_behind(shard, axis, by):
    peers = lax.axis_size(axis)
    return lax.ppermute(shard, axis, [(i, (i + by) % peers) for i in range(peers)])


def select_bits(shifted, current, distances, level):
    chosen = distances >> level & 1 == 1
    return jnp.where(chosen[:, None, None], shifted, current)


def body(orbitals, coulomb, table):
    own_slab = lax.all_gather(orbitals, "lane", axis=1, tiled=True)
    half_loop = lax.axis_size("loop") // 2
    bit_count = half_loop.bit_length()
    slot_count = coulomb.shape[2]
    own_dists = table[0]
    first_move = from_behind(own_slab, "loop", -1)
    fetched = select_bits(first_move[None], own_slab[None], own_dists, 0)
    for level in range(1, bit_count):
        shifted = from_behind(fetched, "loop", -(1 << level))
        fetched = select_bits(shifted, fetched, own_dists, level)
    direct = jnp.zeros(own_slab.shape, jnp.float32)
    back_list = []
    for slot in range(slot_count):
        partner = fetched[slot]
        gram_tile = lax.dot_general(
            own_slab, partner, (((1,), (1,)), ((), ())), preferred_element_type=jnp.float32
        )
        pair_tile = (coulomb[0, 0, slot].astype(jnp.float32) * gram_tile).astype(jnp.bfloat16)
        direct = direct + jnp.dot(pair_tile, partner, preferred_element_type=jnp.float32)
        distance = own_dists[slot]
        weight = jnp.logical_and(distance > 0, distance < half_loop).astype(jnp.float32)
        back_value = lax.dot_general(
            pair_tile, own_slab, (((0,), (0,)), ((), ())), preferred_element_type=jnp.float32
        )
        back_list.append((back_value * weight).astype(jnp.bfloat16))
    back_terms = jnp.stack(back_list)
    for level in range(bit_count):
        shifted = from_behind(back_terms, "loop", 1 << level)
        back_terms = select_bits(shifted, back_terms, own_dists, level)
    summed = direct + jnp.sum(back_terms.astype(jnp.float32), axis=0)
    result = lax.psum_scatter(summed, "lane", scatter_dimension=1, tiled=True)
    return result.astype(jnp.bfloat16)


def solution(mesh):
    in_specs = (P("loop", "lane"), P("loop", "lane", None, None, None), P("lane", None))
    out_specs = P("loop", "lane")
    return jax.shard_map(body, mesh=mesh, in_specs=in_specs, out_specs=out_specs, check_vma=False)
```

profile of v0, /device:TPU:0, one launch (start us, length us, event | category | flops | bytes accessed | tf_op | source)
XLA Modules:
  0.0 268.0 jit_solution(910896911807850899)
XLA Ops:
  6.5 10.2 %all_gather.3 = bf16[512,512]{1,0:T(8,128)(2,1)S(1)} all-gather(bf16[512,256]{1,0:T(8,128)(2,1)} %param.3), channel_id=1, replica_groups=mesh['loop'=16,'lane'=2] {'lane'}, dimensions={1}, use_global_device_ids=true | all-gather | bytes 786432 | tf_op jit(solution)/shard_map/all_gather | solution.py:18
  16.7 3.3 %collective-permute-start = (bf16[512,512]{1,0:T(8,128)(2,1)S(1)}, bf16[512,512]{1,0:T(8,128)(2,1)S(1)}, u32[]{:S(2)}, u32[]{:S(2)}) collective-permute-start(bf16[512,512]{1,0:T(8,128)(2,1)S(1)} %all_gather.3), channel_id=1, source_target_pairs={{0,30},{2,0},{4,2},{6,4},{8,6},{10,8},{12,10},{14,12},{16,14},{18,... | collective-permute-start | bytes 1572872 | tf_op jit(solution)/shard_map/ppermute | solution.py:9
  20.0 0.7 compare_bitcast_fusion.3
  20.7 6.0 %collective-permute-done = bf16[512,512]{1,0:T(8,128)(2,1)S(1)} collective-permute-done((bf16[512,512]{1,0:T(8,128)(2,1)S(1)}, bf16[512,512]{1,0:T(8,128)(2,1)S(1)}, u32[]{:S(2)}, u32[]{:S(2)}) %collective-permute-start) | collective-permute-done | bytes 524320 | tf_op jit(solution)/shard_map/ppermute | solution.py:9
  26.9 1.5 collective-permute-start.1
  28.4 22.3 %collective-permute-done.1 = bf16[2,512,512]{2,1,0:T(8,128)(2,1)S(1)} collective-permute-done((bf16[2,512,512]{2,1,0:T(8,128)(2,1)S(1)}, bf16[2,512,512]{2,1,0:T(8,128)(2,1)S(1)}, u32[]{:S(2)}, u32[]{:S(2)}) %collective-permute-start.1) | collective-permute-done | bytes 1048608 | tf_op jit(solution)/shard_map/ppermute | solution.py:9
  50.9 1.0 collective-permute-start.2
  51.9 24.8 %collective-permute-done.2 = bf16[2,512,512]{2,1,0:T(8,128)(2,1)S(1)} collective-permute-done((bf16[2,512,512]{2,1,0:T(8,128)(2,1)S(1)}, bf16[2,512,512]{2,1,0:T(8,128)(2,1)S(1)}, u32[]{:S(2)}, u32[]{:S(2)}) %collective-permute-start.2) | collective-permute-done | bytes 1048608 | tf_op jit(solution)/shard_map/ppermute | solution.py:9
  76.9 1.0 collective-permute-start.3
  77.9 0.6 fusion.11
  81.6 44.0 %collective-permute-done.3 = bf16[2,512,512]{2,1,0:T(8,128)(2,1)} collective-permute-done((bf16[2,512,512]{2,1,0:T(8,128)(2,1)S(1)}, bf16[2,512,512]{2,1,0:T(8,128)(2,1)}, u32[]{:S(2)}, u32[]{:S(2)}) %collective-permute-start.3) | collective-permute-done | bytes 1048608 | tf_op jit(solution)/shard_map/ppermute | solution.py:9
  125.6 1.4 broadcast_select_fusion.6
  127.0 0.5 fusion.3
  127.5 0.5 fusion.4
  128.0 0.4 fusion.8
  129.0 16.9 %collective-permute-done.4 = bf16[2,512,512]{2,1,0:T(8,128)(2,1)S(1)} collective-permute-done((bf16[2,512,512]{2,1,0:T(8,128)(2,1)S(1)}, bf16[2,512,512]{2,1,0:T(8,128)(2,1)S(1)}, u32[]{:S(2)}, u32[]{:S(2)}) %collective-permute-start.4) | collective-permute-done | bytes 1048608 | tf_op jit(solution)/shard_map/ppermute | solution.py:9
  146.2 23.8 %collective-permute-done.5 = bf16[2,512,512]{2,1,0:T(8,128)(2,1)S(1)} collective-permute-done((bf16[2,512,512]{2,1,0:T(8,128)(2,1)S(1)}, bf16[2,512,512]{2,1,0:T(8,128)(2,1)S(1)}, u32[]{:S(2)}, u32[]{:S(2)}) %collective-permute-start.5) | collective-permute-done | bytes 1048608 | tf_op jit(solution)/shard_map/ppermute | solution.py:9
  170.2 22.9 %collective-permute-done.6 = bf16[2,512,512]{2,1,0:T(8,128)(2,1)S(1)} collective-permute-done((bf16[2,512,512]{2,1,0:T(8,128)(2,1)S(1)}, bf16[2,512,512]{2,1,0:T(8,128)(2,1)S(1)}, u32[]{:S(2)}, u32[]{:S(2)}) %collective-permute-start.6) | collective-permute-done | bytes 1048608 | tf_op jit(solution)/shard_map/ppermute | solution.py:9
  193.4 0.5 fusion.9
  193.9 44.1 %collective-permute-done.7 = bf16[2,512,512]{2,1,0:T(8,128)(2,1)S(1)} collective-permute-done((bf16[2,512,512]{2,1,0:T(8,128)(2,1)S(1)}, bf16[2,512,512]{2,1,0:T(8,128)(2,1)S(1)}, u32[]{:S(2)}, u32[]{:S(2)}) %collective-permute-start.7) | collective-permute-done | bytes 1048608 | tf_op jit(solution)/shard_map/ppermute | solution.py:9
  238.0 0.6 convert_reduce_fusion
  238.5 1.4 fusion.1
  240.0 19.3 %reduce-scatter.2.cloned.1.call-done = f32[512,256]{1,0:T(8,128)} async-done(((f32[512,512]{1,0:T(8,128)}), f32[512,256]{1,0:T(8,128)}) %reduce-scatter.2.cloned.1.call-update) | async-done | bytes 524304 | tf_op jit(solution)/shard_map/reduce_scatter | solution.py:48
  259.3 1.8 convert_element_type.55
  (21 shorter events, 2.4 us)
Async XLA Ops:
  6.5 252.8 %reduce-scatter.2.cloned.1.call-start = ((), (), s32[]{:S(2)}) async-start(), calls=%async_computation.1 | async-start | bytes 1572864 | tf_op jit(solution)/shard_map/reduce_scatter | solution.py:48
  16.7 10.0 %collective-permute-start = (bf16[512,512]{1,0:T(8,128)(2,1)S(1)}, bf16[512,512]{1,0:T(8,128)(2,1)S(1)}, u32[]{:S(2)}, u32[]{:S(2)}) collective-permute-start(bf16[512,512]{1,0:T(8,128)(2,1)S(1)} %all_gather.3), channel_id=1, source_target_pairs={{0,30},{2,0},{4,2},{6,4},{8,6},{10,8},{12,10},{14,12},{16,14},{18,... | collective-permute-start | bytes 1572872 | tf_op jit(solution)/shard_map/ppermute | solution.py:9
  26.9 23.8 %collective-permute-start.1 = (bf16[2,512,512]{2,1,0:T(8,128)(2,1)S(1)}, bf16[2,512,512]{2,1,0:T(8,128)(2,1)S(1)}, u32[]{:S(2)}, u32[]{:S(2)}) collective-permute-start(bf16[2,512,512]{2,1,0:T(8,128)(2,1)S(1)} %broadcast_select_fusion.1), channel_id=1, source_target_pairs={{0,28},{2,30},{4,0},{6,2},{8,4},{10,6},{12,8},{14,10},{16,12},{18,... | collective-permute-start | bytes 3145736 | tf_op jit(solution)/shard_map/ppermute | solution.py:9
  50.9 25.8 %collective-permute-start.2 = (bf16[2,512,512]{2,1,0:T(8,128)(2,1)S(1)}, bf16[2,512,512]{2,1,0:T(8,128)(2,1)S(1)}, u32[]{:S(2)}, u32[]{:S(2)}) collective-permute-start(bf16[2,512,512]{2,1,0:T(8,128)(2,1)S(1)} %broadcast_select_fusion.3), channel_id=1, source_target_pairs={{0,24},{2,26},{4,28},{6,30},{8,0},{10,2},{12,4},{14,6},{16,8},{18,... | collective-permute-start | bytes 3145736 | tf_op jit(solution)/shard_map/ppermute | solution.py:9
  76.7 1.2 copy-start.1
  76.7 4.4 %copy-start = (bf16[1,1,2,512,512]{4,3,2,1,0:T(8,128)(2,1)S(1)}, bf16[1,1,2,512,512]{4,3,2,1,0:T(8,128)(2,1)}, u32[]{:S(2)}) copy-start(bf16[1,1,2,512,512]{4,3,2,1,0:T(8,128)(2,1)} %param.4) | copy-start | bytes 3145732
  76.9 48.7 %collective-permute-start.3 = (bf16[2,512,512]{2,1,0:T(8,128)(2,1)S(1)}, bf16[2,512,512]{2,1,0:T(8,128)(2,1)}, u32[]{:S(2)}, u32[]{:S(2)}) collective-permute-start(bf16[2,512,512]{2,1,0:T(8,128)(2,1)S(1)} %broadcast_select_fusion.5), channel_id=1, source_target_pairs={{0,16},{2,18},{4,20},{6,22},{8,24},{10,26},{12,28},{14,30},{16,0},... | collective-permute-start | bytes 3145736 | tf_op jit(solution)/shard_map/ppermute | solution.py:9
  128.9 17.0 %collective-permute-start.4 = (bf16[2,512,512]{2,1,0:T(8,128)(2,1)S(1)}, bf16[2,512,512]{2,1,0:T(8,128)(2,1)S(1)}, u32[]{:S(2)}, u32[]{:S(2)}) collective-permute-start(bf16[2,512,512]{2,1,0:T(8,128)(2,1)S(1)} %pad_maximum_fusion), channel_id=1, source_target_pairs={{0,2},{2,4},{4,6},{6,8},{8,10},{10,12},{12,14},{14,16},{16,18},{18... | collective-permute-start | bytes 3145736 | tf_op jit(solution)/shard_map/ppermute | solution.py:9
  146.1 23.9 %collective-permute-start.5 = (bf16[2,512,512]{2,1,0:T(8,128)(2,1)S(1)}, bf16[2,512,512]{2,1,0:T(8,128)(2,1)S(1)}, u32[]{:S(2)}, u32[]{:S(2)}) collective-permute-start(bf16[2,512,512]{2,1,0:T(8,128)(2,1)S(1)} %broadcast_select_fusion), channel_id=1, source_target_pairs={{0,4},{2,6},{4,8},{6,10},{8,12},{10,14},{12,16},{14,18},{16,20},{1... | collective-permute-start | bytes 3145736 | tf_op jit(solution)/shard_map/ppermute | solution.py:9
  170.2 23.0 %collective-permute-start.6 = (bf16[2,512,512]{2,1,0:T(8,128)(2,1)S(1)}, bf16[2,512,512]{2,1,0:T(8,128)(2,1)S(1)}, u32[]{:S(2)}, u32[]{:S(2)}) collective-permute-start(bf16[2,512,512]{2,1,0:T(8,128)(2,1)S(1)} %broadcast_select_fusion.2), channel_id=1, source_target_pairs={{0,8},{2,10},{4,12},{6,14},{8,16},{10,18},{12,20},{14,22},{16,24},... | collective-permute-start | bytes 3145736 | tf_op jit(solution)/shard_map/ppermute | solution.py:9
  193.3 44.7 %collective-permute-start.7 = (bf16[2,512,512]{2,1,0:T(8,128)(2,1)S(1)}, bf16[2,512,512]{2,1,0:T(8,128)(2,1)S(1)}, u32[]{:S(2)}, u32[]{:S(2)}) collective-permute-start(bf16[2,512,512]{2,1,0:T(8,128)(2,1)S(1)} %broadcast_select_fusion.4), channel_id=1, source_target_pairs={{0,16},{2,18},{4,20},{6,22},{8,24},{10,26},{12,28},{14,30},{16,0},... | collective-permute-start | bytes 3145736 | tf_op jit(solution)/shard_map/ppermute | solution.py:9
Sparse Core Ops, SparseCore 0:
  240.1 19.1 reduce-scatter.1
where the time goes:
time: 268 us
  waiting for transfers between devices  224 us (84%)
  between operations  16.1 us (6%)
  blocking collectives  10.2 us (4%)
  starting transfers between devices  7.01 us (3%)
  other arithmetic  5.59 us (2%)
  matrix products  3.72 us (1%)
    ppermute x8, waiting for transfers between devices, from_behind(): lax.ppermute(shard, axis, [(i, (i + by) % peers) for i in range(peers)])  205 us
    reduce_scatter x1, waiting for transfers between devices, body(): result = lax.psum_scatter(summed, 'lane', scatter_dimension=1, tiled=True)  19.3 us
    all_gather x1, blocking collectives, body(): own_slab = lax.all_gather(orbitals, 'lane', axis=1, tiled=True)  10.2 us
    ppermute x8, starting transfers between devices, from_behind(): lax.ppermute(shard, axis, [(i, (i + by) % peers) for i in range(peers)])  7.01 us
  transfers between devices with their start and end apart: 9, of which 9 were waited for; matrix products, arithmetic and copies ran while one was open for 1% of the time, Pallas kernels for 0%

commit v1 on v0

--- a/solution.py
+++ b/solution.py
@@ -1,7 +1,14 @@
+import functools
+
 import jax
 import jax.numpy as jnp
 from jax import lax
+from jax.experimental import pallas as pl
+from jax.experimental.pallas import tpu as pltpu
 from jax.sharding import PartitionSpec as P
+
+PIECES = 2
+MESH = pl.DeviceIdType.MESH
 
 
 def from_behind(shard, axis, by):
@@ -14,7 +21,7 @@
     return jnp.where(chosen[:, None, None], shifted, current)
 
 
-def body(orbitals, coulomb, table):
+def general_body(orbitals, coulomb, table):
     own_slab = lax.all_gather(orbitals, "lane", axis=1, tiled=True)
     half_loop = lax.axis_size("loop") // 2
     bit_count = half_loop.bit_length()
@@ -41,7 +48,7 @@
         )
         back_list.append((back_value * weight).astype(jnp.bfloat16))
     back_terms = jnp.stack(back_list)
-    for level in range(bit_count):
+    for level in range(bit_count - 1):
         shifted = from_behind(back_terms, "loop", 1 << level)
         back_terms = select_bits(shifted, back_terms, own_dists, level)
     summed = direct + jnp.sum(back_terms.astype(jnp.float32), axis=0)
@@ -49,7 +56,284 @@
     return result.astype(jnp.bfloat16)
 
 
+def pick(items, index):
+    value = items[-1]
+    for i in range(len(items) - 2, -1, -1):
+        value = jnp.where(index == i, items[i], value)
+    return value
+
+
+def kernel(
+    n_loop, h_ref, c_ref, t_ref, out_ref,
+    slab, tiles, tab_out, tab_in, pools, y_out, sel, b_out, b_in,
+    same, core_out, core_in, z_out, z_in, x_out, x_in, direct, d_out, d_in,
+    stack, fin, send, recv, local,
+):
+    half_loop = n_loop // 2
+    me = lax.axis_index("loop")
+    x = lax.axis_index("lane")
+    ox = 1 - x
+    c = me % 2
+    y = (me // 2) % 2
+    z4 = (me // 4) * 4
+    low = me - z4
+    points, width = h_ref.shape
+    rows = points // 2
+    chunk = rows // PIECES
+    bf16, f32 = jnp.bfloat16, jnp.float32
+
+    def at_z(step):
+        return ((z4 + 4 * step) % n_loop + low, x)
+
+    across = (me, ox)
+    core = (me + 1 - 2 * c, x)
+    over_y = (me + 2 - 4 * y, x)
+
+    counter = [0]
+
+    def remote(src, dst, to):
+        i = counter[0]
+        counter[0] += 1
+        copy = pltpu.make_async_remote_copy(
+            src_ref=src, dst_ref=dst, send_sem=send.at[i], recv_sem=recv.at[i],
+            device_id=to, device_id_type=MESH,
+        )
+        copy.start()
+        started.append(copy)
+        return copy
+
+    started = []
+
+    barrier = pltpu.get_barrier_semaphore()
+    for peer in (across, core, over_y, at_z(1), at_z(2), at_z(3)):
+        pl.semaphore_signal(barrier, inc=1, device_id=peer, device_id_type=MESH)
+    pl.semaphore_wait(barrier, 6)
+
+    my_cols = pl.ds(pl.multiple_of(x * width, width), width)
+    other_cols = pl.ds(pl.multiple_of(ox * width, width), width)
+    my_rows = pl.ds(pl.multiple_of(x * rows, rows), rows)
+    other_rows = pl.ds(pl.multiple_of(ox * rows, rows), rows)
+
+    def my_chunk(k):
+        return pl.ds(pl.multiple_of(x * rows + k * chunk, chunk), chunk)
+
+    def other_chunk(k):
+        return pl.ds(pl.multiple_of(ox * rows + k * chunk, chunk), chunk)
+
+    piece_in = [
+        remote(h_ref.at[other_chunk(k)], pools[k].at[c, :, my_cols], across)
+        for k in range(PIECES)
+    ]
+    for s in range(2):
+        tab_out[s] = jnp.full(tab_out.shape[1:], t_ref[0, s], jnp.int32)
+    table_in = remote(tab_out, tab_in, across)
+    for k in range(PIECES):
+        pools[k][c, :, my_cols] = h_ref[my_chunk(k)]
+    slab_in = remote(h_ref.at[my_rows], slab.at[my_rows, my_cols], across)
+    tile_in = [
+        remote(c_ref.at[0, 0, s, :, other_cols], tiles.at[2 * x + s], across) for s in range(2)
+    ]
+    tile_own = []
+    for s in range(2):
+        copy = pltpu.make_async_copy(c_ref.at[0, 0, s, :, my_cols], tiles.at[2 * x + s], local.at[s])
+        copy.start()
+        tile_own.append(copy)
+
+    z_move, core_move = [], []
+    for k in range(PIECES):
+        piece_in[k].wait_recv()
+        z_move.append([
+            remote(pools[k].at[c], pools[k].at[2 * step + c], at_z(4 - step)) for step in (1, 2)
+        ])
+        core_move.append([remote(pools[k].at[c], pools[k].at[c], core)])
+
+    slab[other_rows, my_cols] = h_ref[other_rows]
+    for k in range(PIECES):
+        slab[my_chunk(k), :] = pools[k][c]
+
+    table_in.wait_recv()
+    mine = [t_ref[0, s] for s in range(2)]
+    theirs = [jnp.max(tab_in[s]) for s in range(2)]
+    first = x == 0
+    dist = [jnp.where(first, mine[s], theirs[s]) for s in range(2)]
+    dist += [jnp.where(first, theirs[s], mine[s]) for s in range(2)]
+    inner = [jnp.logical_and(d != 0, d != half_loop) for d in dist]
+    slot_zero = pick([jnp.int32(i) for i in range(4)], jnp.int32(-1))
+    slot_half = slot_zero
+    for i in range(3):
+        slot_zero = jnp.where(dist[i] == 0, i, slot_zero)
+        slot_half = jnp.where(dist[i] == half_loop, i, slot_half)
+    slot_a = jnp.where(inner[0], 0, jnp.where(inner[1], 1, 2))
+    slot_b = jnp.where(inner[3], 3, jnp.where(inner[2], 2, 1))
+    inner_slots = (slot_a, slot_b)
+    inner_dist = [pick(dist, s) for s in inner_slots]
+    own_at = [low + d for d in inner_dist]
+    next_at = [low + 2 - 4 * y + d for d in inner_dist]
+
+    def spot(at):
+        return (at >> 2) * 2 + (at & 1)
+
+    def here(at):
+        return ((at >> 1) & 1) ^ y
+
+    y_move = []
+    for k in range(PIECES):
+        for step in (1, 2):
+            z_move[k][step - 1].wait_recv()
+            core_move[k].append(
+                remote(pools[k].at[2 * step + c], pools[k].at[2 * step + c], core)
+            )
+        for copy in core_move[k]:
+            copy.wait_recv()
+        for j in range(2):
+            y_out[k][j] = pools[k][spot(next_at[j])]
+        y_move.append(remote(y_out[k], sel[k].at[pl.ds(2, 2)], over_y))
+        for j in range(2):
+            sel[k][j] = pools[k][spot(own_at[j])]
+
+    slab_in.wait_recv()
+    for copy in tile_own:
+        copy.wait()
+    for copy in tile_in:
+        copy.wait_recv()
+
+    b_move = []
+    for k in range(PIECES):
+        stack[pl.ds(0, chunk)] = pools[k][c]
+        stack[pl.ds(chunk, chunk)] = pools[k][4 + c]
+        y_move[k].wait_recv()
+        for j in range(2):
+            stack[pl.ds((2 + j) * chunk, chunk)] = sel[k][j + 2 * here(own_at[j])]
+        gram = lax.dot_general(
+            slab[...], stack[...], (((1,), (1,)), ((), ())), preferred_element_type=f32
+        )
+        held = jnp.concatenate(
+            [tiles[s, :, pl.ds(k * chunk, chunk)] for s in (slot_zero, slot_half) + inner_slots],
+            axis=1,
+        )
+        pair = (held.astype(f32) * gram).astype(bf16)
+        back = lax.dot_general(
+            pair[:, 2 * chunk:], slab[...], (((0,), (0,)), ((), ())), preferred_element_type=f32
+        ).astype(bf16)
+        for j in range(2):
+            b_out[k][j] = back[j * chunk:(j + 1) * chunk]
+        b_move.append(remote(b_out[k], b_in[k], over_y))
+        part = jnp.dot(pair, stack[...], preferred_element_type=f32)
+        if k == 0:
+            direct[...] = part
+        else:
+            direct[...] += part
+    d_out[...] = direct[:, other_cols].astype(bf16)
+    direct_move = remote(d_out, d_in, across)
+
+    def mask(at, plane, side):
+        fits = jnp.logical_and(here(at) == 0, spot(at) == plane * 2 + side)
+        return jnp.where(fits, 1.0, 0.0).astype(f32)
+
+    b_core, b_z = [], []
+    for k in range(PIECES):
+        b_move[k].wait_recv()
+        for plane in range(3):
+            keep = jnp.zeros((chunk, 2 * width), f32)
+            give = jnp.zeros((chunk, 2 * width), f32)
+            for j in range(2):
+                for at, src in ((own_at[j], b_out[k]), (next_at[j], b_in[k])):
+                    value = src[j].astype(f32)
+                    keep += value * mask(at, plane, c)
+                    give += value * mask(at, plane, 1 - c)
+            same[k][plane] = keep
+            core_out[k][plane] = give.astype(bf16)
+        b_core.append(remote(core_out[k], core_in[k], core))
+    for k in range(PIECES):
+        b_core[k].wait_recv()
+        moves = []
+        for step in (2, 1):
+            z_out[k][step - 1] = (same[k][step] + core_in[k][step].astype(f32)).astype(bf16)
+            moves.append(remote(z_out[k].at[step - 1], z_in[k].at[step - 1], at_z(step)))
+        b_z.append(moves)
+    last = []
+    for k in range(PIECES):
+        for copy in b_z[k]:
+            copy.wait_recv()
+        fin[k] = (
+            same[k][0] + core_in[k][0].astype(f32)
+            + z_in[k][0].astype(f32) + z_in[k][1].astype(f32)
+        )
+        x_out[k][...] = fin[k, :, other_cols].astype(bf16)
+        last.append(remote(x_out[k], x_in[k], across))
+    direct_move.wait_recv()
+    for k in range(PIECES):
+        r = my_chunk(k)
+        out_ref[r, :] = (
+            direct[r, my_cols] + d_in[r, :].astype(f32) + fin[k, :, my_cols]
+        ).astype(bf16)
+    for k in range(PIECES):
+        last[k].wait_recv()
+        r = other_chunk(k)
+        out_ref[r, :] = (
+            direct[r, my_cols] + d_in[r, :].astype(f32) + x_in[k][...].astype(f32)
+        ).astype(bf16)
+    for copy in started:
+        copy.wait_send()
+
+
+COPIES = 4 + 1 + 12 * PIECES
+
+
+def planned_body(n_loop, orbitals, coulomb, table):
+    points, width = orbitals.shape
+    rows, full = points // 2, 2 * width
+    chunk = rows // PIECES
+    bf16, f32 = jnp.bfloat16, jnp.float32
+
+    def each(shape, dtype=bf16):
+        return [pltpu.VMEM(shape, dtype) for _ in range(PIECES)]
+
+    return pl.pallas_call(
+        functools.partial(kernel, n_loop),
+        out_shape=jax.ShapeDtypeStruct(orbitals.shape, bf16),
+        in_specs=[
+            pl.BlockSpec(memory_space=pltpu.VMEM),
+            pl.BlockSpec(memory_space=pltpu.VMEM),
+            pl.BlockSpec(memory_space=pltpu.SMEM),
+        ],
+        out_specs=pl.BlockSpec(memory_space=pltpu.VMEM),
+        scratch_shapes=[
+            pltpu.VMEM((points, full), bf16),
+            pltpu.VMEM((4, points, rows), bf16),
+            pltpu.VMEM((2, 8, 128), jnp.int32),
+            pltpu.VMEM((2, 8, 128), jnp.int32),
+            each((6, chunk, full)),
+            each((2, chunk, full)),
+            each((4, chunk, full)),
+            each((2, chunk, full)),
+            each((2, chunk, full)),
+            each((3, chunk, full), f32),
+            each((3, chunk, full)),
+            each((3, chunk, full)),
+            each((2, chunk, full)),
+            each((2, chunk, full)),
+            each((chunk, width)),
+            each((chunk, width)),
+            pltpu.VMEM((points, full), f32),
+            pltpu.VMEM((points, width), bf16),
+            pltpu.VMEM((points, width), bf16),
+            pltpu.VMEM((4 * chunk, full), bf16),
+            pltpu.VMEM((PIECES, chunk, full), f32),
+            pltpu.SemaphoreType.DMA((COPIES,)),
+            pltpu.SemaphoreType.DMA((COPIES,)),
+            pltpu.SemaphoreType.DMA((2,)),
+        ],
+        compiler_params=pltpu.CompilerParams(
+            collective_id=0, has_side_effects=True, vmem_limit_bytes=48 * 1024 * 1024
+        ),
+    )(orbitals, coulomb, table)
+
+
 def solution(mesh):
     in_specs = (P("loop", "lane"), P("loop", "lane", None, None, None), P("lane", None))
     out_specs = P("loop", "lane")
+    n_loop, n_lane = mesh.shape["loop"], mesh.shape["lane"]
+    fits = n_loop == 4 * 4 and n_lane == 2
+    body = functools.partial(planned_body, n_loop) if fits else general_body
     return jax.shard_map(body, mesh=mesh, in_specs=in_specs, out_specs=out_specs, check_vma=False)

time: 268 us -> 72.4 us (0.27)
  waiting for transfers between devices: 224 us -> 0 us
  Pallas kernels: 0 us -> 68.7 us
  between operations: 16.1 us -> 0.01 us
  blocking collectives: 10.2 us -> 0 us
  starting transfers between devices: 7.01 us -> 0 us
  other arithmetic: 5.59 us -> 0 us
  matrix products: 3.72 us -> 0 us
    ppermute x8 -> x0, waiting for transfers between devices: 205 us -> none  [from_behind(): lax.ppermute(shard, axis, [(i, (i + by) % peers) for i in range(peers)])]
    pallas_call x0 -> x1, Pallas kernels: none -> 68.7 us  [planned_body(): pl.pallas_call(functools.partial(kernel, n_loop), out_shape=jax.ShapeDtyp...]
    reduce_scatter x1 -> x0, waiting for transfers between devices: 19.3 us -> none  [body(): result = lax.psum_scatter(summed, 'lane', scatter_dimension=1, tiled=True)]
    all_gather x1 -> x0, blocking collectives: 10.2 us -> none  [body(): own_slab = lax.all_gather(orbitals, 'lane', axis=1, tiled=True)]
    ppermute x8 -> x0, starting transfers between devices: 7.01 us -> none  [from_behind(): lax.ppermute(shard, axis, [(i, (i + by) % peers) for i in range(peers)])]
    dot_general x6 -> x0, matrix products: 3.72 us -> none  [the longest x2 1.9 us: body(): jnp.dot(pair_tile, partner, preferred_element_type=jnp.float32)]
    unnamed x6 -> x7, local copies, waits for them, and re-layouts: 0.43 us -> 3.53 us
  transfers between devices with their start and end apart: 9 -> 0, of which waited for: 9 -> 0; matrix products, arithmetic and copies ran while one was open for 1% -> 0% of each run, Pallas kernels for 0% -> 0%
where the time goes in v1:
time: 72.4 us; the launch traced here: 72.3 us
  Pallas kernels  68.7 us (95%)
  local copies, waits for them, and re-layouts  3.53 us (5%)
    pallas_call x1, Pallas kernels, planned_body(): pl.pallas_call(functools.partial(kernel, n_loop), out_shape=jax.ShapeDtyp...  68.7 us
    unnamed x7, local copies, waits for them, and re-layouts  3.53 us

profile of v1, /device:TPU:0, one launch (start us, length us, event | category | flops | bytes accessed | tf_op | source)
XLA Modules:
  0.0 72.3 jit_solution(5734710955716518678)
XLA Ops:
  0.0 0.0 copy-start
  0.0 1.2 %copy-done = bf16[1,1,2,512,512]{4,3,2,1,0:T(8,128)(2,1)S(1)} copy-done((bf16[1,1,2,512,512]{4,3,2,1,0:T(8,128)(2,1)S(1)}, bf16[1,1,2,512,512]{4,3,2,1,0:T(8,128)(2,1)}, u32[]{:S(2)}) %copy-start) | copy-done | bytes 1048600
  1.2 0.0 copy-start.1
  1.2 0.9 %copy-done.1 = bf16[512,256]{1,0:T(8,128)(2,1)S(1)} copy-done((bf16[512,256]{1,0:T(8,128)(2,1)S(1)}, bf16[512,256]{1,0:T(8,128)(2,1)}, u32[]{:S(2)}) %copy-start.1) | copy-done | bytes 262168
  2.2 0.0 copy-start.2
  2.2 0.7 copy-done.2
  2.8 68.7 %shard_map.37 = bf16[512,256]{1,0:T(8,128)(2,1)S(1)} custom-call(bf16[512,256]{1,0:T(8,128)(2,1)S(1)} %copy-done.1, bf16[1,1,2,512,512]{4,3,2,1,0:T(8,128)(2,1)S(1)} %copy-done, s32[1,2]{1,0:T(1,128)S(1)} %copy-done.2), custom_call_target="tpu_custom_call" | custom-call | tf_op jit(solution)/shard_map/pallas_call | solution.py:292
  71.6 0.7 copy.5
Async XLA Ops:
  0.0 1.2 %copy-start = (bf16[1,1,2,512,512]{4,3,2,1,0:T(8,128)(2,1)S(1)}, bf16[1,1,2,512,512]{4,3,2,1,0:T(8,128)(2,1)}, u32[]{:S(2)}) copy-start(bf16[1,1,2,512,512]{4,3,2,1,0:T(8,128)(2,1)} %c_ref.1) | copy-start | bytes 3145732
  1.2 0.9 %copy-start.1 = (bf16[512,256]{1,0:T(8,128)(2,1)S(1)}, bf16[512,256]{1,0:T(8,128)(2,1)}, u32[]{:S(2)}) copy-start(bf16[512,256]{1,0:T(8,128)(2,1)} %h_ref.1) | copy-start | bytes 786436
  2.2 0.7 copy-start.2

commit v2 on v1

v2 whole, which is shorter than its diff:
```python
import functools

import jax
import jax.numpy as jnp
from jax import lax
from jax.experimental import pallas as pl
from jax.experimental.pallas import tpu as pltpu
from jax.sharding import PartitionSpec as P

PIECES = 4
PARTS = 2
MESH = pl.DeviceIdType.MESH


def from_behind(shard, axis, by):
    peers = lax.axis_size(axis)
    return lax.ppermute(shard, axis, [(i, (i + by) % peers) for i in range(peers)])


def select_bits(shifted, current, distances, level):
    chosen = distances >> level & 1 == 1
    return jnp.where(chosen[:, None, None], shifted, current)


def general_body(orbitals, coulomb, table):
    own_slab = lax.all_gather(orbitals, "lane", axis=1, tiled=True)
    half_loop = lax.axis_size("loop") // 2
    bit_count = half_loop.bit_length()
    slot_count = coulomb.shape[2]
    own_dists = table[0]
    first_move = from_behind(own_slab, "loop", -1)
    fetched = select_bits(first_move[None], own_slab[None], own_dists, 0)
    for level in range(1, bit_count):
        shifted = from_behind(fetched, "loop", -(1 << level))
        fetched = select_bits(shifted, fetched, own_dists, level)
    direct = jnp.zeros(own_slab.shape, jnp.float32)
    back_list = []
    for slot in range(slot_count):
        partner = fetched[slot]
        gram_tile = lax.dot_general(
            own_slab, partner, (((1,), (1,)), ((), ())), preferred_element_type=jnp.float32
        )
        pair_tile = (coulomb[0, 0, slot].astype(jnp.float32) * gram_tile).astype(jnp.bfloat16)
        direct = direct + jnp.dot(pair_tile, partner, preferred_element_type=jnp.float32)
        distance = own_dists[slot]
        weight = jnp.logical_and(distance > 0, distance < half_loop).astype(jnp.float32)
        back_value = lax.dot_general(
            pair_tile, own_slab, (((0,), (0,)), ((), ())), preferred_element_type=jnp.float32
        )
        back_list.append((back_value * weight).astype(jnp.bfloat16))
    back_terms = jnp.stack(back_list)
    for level in range(bit_count - 1):
        shifted = from_behind(back_terms, "loop", 1 << level)
        back_terms = select_bits(shifted, back_terms, own_dists, level)
    summed = direct + jnp.sum(back_terms.astype(jnp.float32), axis=0)
    result = lax.psum_scatter(summed, "lane", scatter_dimension=1, tiled=True)
    return result.astype(jnp.bfloat16)


def pick(items, index):
    value = items[-1]
    for i in range(len(items) - 2, -1, -1):
        value = jnp.where(index == i, items[i], value)
    return value


def kernel(
    n_loop, h_ref, c_ref, t_ref, out_ref,
    slab, tiles, tab_out, tab_in, pools, y_out, sel, cand,
    same, core_out, core_in, z_out, z_in, z_via, x_out, x_in, direct, d_out, d_in,
    stack, fin, send, recv, local,
):
    half_loop = n_loop // 2
    me = lax.axis_index("loop")
    x = lax.axis_index("lane")
    ox = 1 - x
    c = me % 2
    y = (me // 2) % 2
    z = me // 4
    low = me - z * 4
    points, width = h_ref.shape
    rows = points // 2
    chunk = rows // PIECES
    part_cols = rows // PARTS
    per_part = PIECES // PARTS
    bf16, f32 = jnp.bfloat16, jnp.float32

    def at_z(step):
        return ((z * 4 + 4 * step) % n_loop + low, x)

    across = (me, ox)
    core = (me + 1 - 2 * c, x)
    over_y = (me + 2 - 4 * y, x)

    sems = {}

    def sem_of(name):
        return sems.setdefault(name, len(sems))

    started = []

    def remote(name, src, dst, to, lands=None, when=None):
        copy = pltpu.make_async_remote_copy(
            src_ref=src, dst_ref=dst, send_sem=send.at[sem_of(name)],
            recv_sem=recv.at[sem_of(lands or name)], device_id=to, device_id_type=MESH,
        )
        if when is None:
            copy.start()
        else:
            pl.when(when)(copy.start)
        started.append((copy, when))
        return copy

    my_cols = pl.ds(pl.multiple_of(x * width, width), width)
    other_cols = pl.ds(pl.multiple_of(ox * width, width), width)
    my_rows = pl.ds(pl.multiple_of(x * rows, rows), rows)
    other_rows = pl.ds(pl.multiple_of(ox * rows, rows), rows)

    def my_chunk(k):
        return pl.ds(pl.multiple_of(x * rows + k * chunk, chunk), chunk)

    def other_chunk(k):
        return pl.ds(pl.multiple_of(ox * rows + k * chunk, chunk), chunk)

    def tile_cols(half, lane):
        return pl.ds(pl.multiple_of(lane * rows + half * part_cols, part_cols), part_cols)

    own_copies, slab_own = [], []
    for k in range(PIECES):
        copy = pltpu.make_async_copy(
            h_ref.at[my_chunk(k)], pools[k].at[c, :, my_cols], local.at[k]
        )
        copy.start()
        own_copies.append(copy)
    copy = pltpu.make_async_copy(h_ref, slab.at[:, my_cols], local.at[PIECES])
    copy.start()
    slab_own.append(copy)
    for half in range(PARTS):
        for s in range(2):
            copy = pltpu.make_async_copy(
                c_ref.at[0, 0, s, :, tile_cols(half, x)], tiles[half].at[2 * x + s],
                local.at[PIECES + 1 + 2 * half + s],
            )
            copy.start()
            slab_own.append(copy)
    for s in range(2):
        tab_out[s] = jnp.full(tab_out.shape[1:], t_ref[0, s], jnp.int32)
    for k in range(PIECES):
        cand[k][4] = jnp.zeros(cand[k].shape[1:], bf16)

    @pl.when(z == 0)
    def _():
        for k in range(PIECES):
            z_in[k][0] = jnp.zeros(z_in[k].shape[1:], bf16)

    @pl.when(z == 2)
    def _():
        for k in range(PIECES):
            z_in[k][1] = jnp.zeros(z_in[k].shape[1:], bf16)

    barrier = pltpu.get_barrier_semaphore()
    for peer in (across, core, over_y, at_z(1), at_z(2), at_z(3)):
        pl.semaphore_signal(barrier, inc=1, device_id=peer, device_id_type=MESH)
    pl.semaphore_wait(barrier, 6)

    piece_in = [
        remote(("piece", k), h_ref.at[other_chunk(k)], pools[k].at[c, :, my_cols], across)
        for k in range(PIECES)
    ]
    table_in = remote(("table",), tab_out, tab_in, across)

    z_move, core_move = [], []
    for k in range(PIECES):
        own_copies[k].wait()
        piece_in[k].wait_recv()
        one = remote(
            ("z1", k), pools[k].at[c], pools[k].at[2 + c], at_z(3), when=z != 0
        )
        two = remote(
            ("z2", k), pools[k].at[c], pools[k].at[4 + c], at_z(2), when=z != 2
        )
        z_move.append((one, two))
        core_move.append([remote(("c0", k), pools[k].at[c], pools[k].at[c], core)])
    slab_in = remote(("slab",), h_ref.at[my_rows], slab.at[my_rows, my_cols], across)

    def send_tiles(half):
        return [
            remote(
                ("tile", half, s), c_ref.at[0, 0, s, :, tile_cols(half, ox)],
                tiles[half].at[2 * x + s], across,
            )
            for s in range(2)
        ]

    tile_in = [send_tiles(half) for half in range(1)]

    table_in.wait_recv()
    mine = [t_ref[0, s] for s in range(2)]
    theirs = [jnp.max(tab_in[s]) for s in range(2)]
    first = x == 0
    dist = [jnp.where(first, mine[s], theirs[s]) for s in range(2)]
    dist += [jnp.where(first, theirs[s], mine[s]) for s in range(2)]
    inner = [jnp.logical_and(d != 0, d != half_loop) for d in dist]
    slot_zero = jnp.int32(3)
    slot_half = slot_zero
    for i in range(3):
        slot_zero = jnp.where(dist[i] == 0, i, slot_zero)
        slot_half = jnp.where(dist[i] == half_loop, i, slot_half)
    slot_a = jnp.where(inner[0], 0, jnp.where(inner[1], 1, 2))
    slot_b = jnp.where(inner[3], 3, jnp.where(inner[2], 2, 1))
    inner_slots = (slot_a, slot_b)
    inner_dist = [pick(dist, s) for s in inner_slots]
    own_at = [low + d for d in inner_dist]
    next_at = [low + 2 - 4 * y + d for d in inner_dist]

    def spot(at):
        return (at >> 2) * 2 + (at & 1)

    def here(at):
        return ((at >> 1) & 1) ^ y

    def source(j, plane, side):
        want = plane * 2 + side
        own = jnp.logical_and(here(own_at[j]) == 0, spot(own_at[j]) == want)
        near = jnp.logical_and(here(next_at[j]) == 0, spot(next_at[j]) == want)
        return jnp.where(own, j, jnp.where(near, 2 + j, 4))

    y_move, b_move, b_core, b_z, last = [], [], [], [], []

    def gather_rows(k):
        for step in (1, 2):
            z_move[k][step - 1].wait_recv()
            if step == 1:
                remote(
                    ("via1", k), pools[k].at[2 + c], pools[k].at[4 + c], at_z(3),
                    lands=("z2", k), when=z == 1,
                )
            else:
                remote(
                    ("via2", k), pools[k].at[4 + c], pools[k].at[2 + c], at_z(1),
                    lands=("z1", k), when=z == 2,
                )
            core_move[k].append(
                remote(
                    ("c", step, k), pools[k].at[2 * step + c], pools[k].at[2 * step + c], core
                )
            )
        for copy in core_move[k]:
            copy.wait_recv()
        for j in range(2):
            y_out[k][j] = pools[k][spot(next_at[j])]
        y_move.append(remote(("y", k), y_out[k], sel[k].at[pl.ds(2, 2)], over_y))
        for j in range(2):
            sel[k][j] = pools[k][spot(own_at[j])]

    def compute(k):
        half = k // per_part
        if k == 0:
            for copy in slab_own:
                copy.wait()
            for i in range(PIECES):
                slab[my_chunk(i), other_cols] = pools[i][c, :, other_cols]
            slab_in.wait_recv()
        if k % per_part == 0:
            for copy in tile_in[half]:
                copy.wait_recv()
        stack[pl.ds(0, chunk)] = pools[k][c]
        stack[pl.ds(chunk, chunk)] = pools[k][4 + c]
        y_move[k].wait_recv()
        for j in range(2):
            stack[pl.ds((2 + j) * chunk, chunk)] = sel[k][j + 2 * here(own_at[j])]
        gram = lax.dot_general(
            slab[...], stack[...], (((1,), (1,)), ((), ())), preferred_element_type=f32
        )
        at = (k % per_part) * chunk
        held = jnp.concatenate(
            [tiles[half][s, :, at:at + chunk] for s in (slot_zero, slot_half) + inner_slots],
            axis=1,
        )
        pair = (held.astype(f32) * gram).astype(bf16)
        back = lax.dot_general(
            pair[:, 2 * chunk:], slab[...], (((0,), (0,)), ((), ())), preferred_element_type=f32
        ).astype(bf16)
        for j in range(2):
            cand[k][j] = back[j * chunk:(j + 1) * chunk]
        b_move.append(
            remote(("b", k), cand[k].at[pl.ds(0, 2)], cand[k].at[pl.ds(2, 2)], over_y)
        )
        part = jnp.dot(pair, stack[...], preferred_element_type=f32)
        if k == 0:
            direct[...] = part
        else:
            direct[...] += part
        if k == PIECES - 1:
            d_out[...] = direct[:, other_cols].astype(bf16)
            last.append(remote(("direct",), d_out, d_in, across))

    def sort_back(k):
        b_move[k].wait_recv()
        for plane in (2, 1, 0):
            for side, keep in ((1 - c, False), (c, True)):
                a, b = (cand[k][source(j, plane, side)].astype(f32) for j in range(2))
                if keep:
                    same[k][plane] = a + b
                else:
                    core_out[k][plane] = (a + b).astype(bf16)
        b_core.append(remote(("bc", k), core_out[k], core_in[k], core))

    def send_back(k):
        b_core[k].wait_recv()

        def total(step):
            return same[k][step] + core_in[k][step].astype(f32)

        for step in (1, 2):
            z_out[k][step - 1] = total(step).astype(bf16)
        one, two = z_out[k].at[0], z_out[k].at[1]
        via = remote(("v0", k), two, z_via[k], at_z(1), lands=("v", k), when=z == 0)
        remote(("v3", k), one, z_via[k], at_z(3), lands=("v", k), when=z == 3)
        z_a = remote(
            ("ba", k), one, z_in[k].at[0], at_z(1), lands=("bz1", k),
            when=jnp.logical_or(z == 0, z == 2),
        )
        z_b = remote(
            ("bb", k), two, z_in[k].at[1], at_z(2), lands=("bz2", k),
            when=jnp.logical_or(z == 1, z == 3),
        )

        @pl.when(z == 1)
        def _():
            via.wait_recv()
            z_out[k][0] = (total(1) + z_via[k][...].astype(f32)).astype(bf16)

        @pl.when(z == 2)
        def _():
            via.wait_recv()
            z_out[k][1] = (total(2) + z_via[k][...].astype(f32)).astype(bf16)

        remote(("bc1", k), one, z_in[k].at[0], at_z(1), lands=("bz1", k), when=z == 1)
        remote(("bc2", k), two, z_in[k].at[1], at_z(2), lands=("bz2", k), when=z == 2)
        b_z.append((z_a, z_b))

    def finish(k):
        pl.when(z != 0)(b_z[k][0].wait_recv)
        pl.when(z != 2)(b_z[k][1].wait_recv)
        fin[k] = (
            same[k][0] + core_in[k][0].astype(f32)
            + z_in[k][0].astype(f32) + z_in[k][1].astype(f32)
        )
        x_out[k][...] = fin[k, :, other_cols].astype(bf16)
        last.append(remote(("x", k), x_out[k], x_in[k], across))

    for t in range(PIECES + 4):
        for lag, step in enumerate((gather_rows, compute, sort_back, send_back, finish)):
            if 0 <= t - lag < PIECES:
                step(t - lag)
        if t + 1 < PARTS:
            tile_in.append(send_tiles(t + 1))

    last[0].wait_recv()
    for k in range(PIECES):
        r = my_chunk(k)
        out_ref[r, :] = (
            direct[r, my_cols] + d_in[r, :].astype(f32) + fin[k, :, my_cols]
        ).astype(bf16)
    for k in range(PIECES):
        last[k + 1].wait_recv()
        r = other_chunk(k)
        out_ref[r, :] = (
            direct[r, my_cols] + d_in[r, :].astype(f32) + x_in[k][...].astype(f32)
        ).astype(bf16)
    for copy, when in started:
        if when is None:
            copy.wait_send()
        else:
            pl.when(when)(copy.wait_send)


COPIES = 3 + 2 * PARTS + 24 * PIECES


def planned_body(n_loop, orbitals, coulomb, table):
    points, width = orbitals.shape
    rows, full = points // 2, 2 * width
    chunk = rows // PIECES
    bf16, f32 = jnp.bfloat16, jnp.float32

    def each(shape, dtype=bf16, count=PIECES):
        return [pltpu.VMEM(shape, dtype) for _ in range(count)]

    return pl.pallas_call(
        functools.partial(kernel, n_loop),
        out_shape=jax.ShapeDtypeStruct(orbitals.shape, bf16),
        in_specs=[
            pl.BlockSpec(memory_space=pltpu.HBM),
            pl.BlockSpec(memory_space=pltpu.HBM),
            pl.BlockSpec(memory_space=pltpu.SMEM),
        ],
        out_specs=pl.BlockSpec(memory_space=pltpu.VMEM),
        scratch_shapes=[
            pltpu.VMEM((points, full), bf16),
            each((4, points, rows // PARTS), count=PARTS),
            pltpu.VMEM((2, 8, 128), jnp.int32),
            pltpu.VMEM((2, 8, 128), jnp.int32),
            each((6, chunk, full)),
            each((2, chunk, full)),
            each((4, chunk, full)),
            each((5, chunk, full)),
            each((3, chunk, full), f32),
            each((3, chunk, full)),
            each((3, chunk, full)),
            each((2, chunk, full)),
            each((2, chunk, full)),
            each((chunk, full)),
            each((chunk, width)),
            each((chunk, width)),
            pltpu.VMEM((points, full), f32),
            pltpu.VMEM((points, width), bf16),
            pltpu.VMEM((points, width), bf16),
            pltpu.VMEM((4 * chunk, full), bf16),
            pltpu.VMEM((PIECES, chunk, full), f32),
            pltpu.SemaphoreType.DMA((COPIES,)),
            pltpu.SemaphoreType.DMA((COPIES,)),
            pltpu.SemaphoreType.DMA((PIECES + 1 + 2 * PARTS,)),
        ],
        compiler_params=pltpu.CompilerParams(
            collective_id=0, has_side_effects=True, vmem_limit_bytes=63 * 1024 * 1024
        ),
    )(orbitals, coulomb, table)


def solution(mesh):
    in_specs = (P("loop", "lane"), P("loop", "lane", None, None, None), P("lane", None))
    out_specs = P("loop", "lane")
    n_loop, n_lane = mesh.shape["loop"], mesh.shape["lane"]
    fits = n_loop == 4 * 4 and n_lane == 2
    body = functools.partial(planned_body, n_loop) if fits else general_body
    return jax.shard_map(body, mesh=mesh, in_specs=in_specs, out_specs=out_specs, check_vma=False)
```

time: 72.4 us -> 65.6 us (0.906)
  Pallas kernels: 68.7 us -> 63.7 us
  local copies, waits for them, and re-layouts: 3.53 us -> 1.67 us
    pallas_call x1, Pallas kernels: 68.7 us -> 63.7 us  [planned_body(): pl.pallas_call(functools.partial(kernel, n_loop), out_shape=jax.ShapeDtyp...]
    unnamed x7 -> x1, local copies, waits for them, and re-layouts: 3.53 us -> 1.67 us
where the time goes in v2:
time: 65.6 us; the launch traced here: 65.4 us
  Pallas kernels  63.7 us (97%)
  local copies, waits for them, and re-layouts  1.67 us (3%)
    pallas_call x1, Pallas kernels, planned_body(): pl.pallas_call(functools.partial(kernel, n_loop), out_shape=jax.ShapeDtyp...  63.7 us
    unnamed x1, local copies, waits for them, and re-layouts  1.67 us

profile of v2, /device:TPU:0, one launch (start us, length us, event | category | flops | bytes accessed | tf_op | source)
XLA Modules:
  0.0 65.4 jit_solution(381145862478179612)
XLA Ops:
  0.0 63.7 %shard_map.37 = bf16[512,256]{1,0:T(8,128)(2,1)} custom-call(bf16[512,256]{1,0:T(8,128)(2,1)} %h_ref.1, bf16[1,1,2,512,512]{4,3,2,1,0:T(8,128)(2,1)} %c_ref.1, s32[1,2]{1,0:T(1,128)} %t_ref.1), custom_call_target="tpu_custom_call" | custom-call | tf_op jit(solution)/shard_map/pallas_call | solution.py:391
  63.7 1.7 %copy.5 = bf16[512,256]{1,0:T(8,128)(2,1)} copy(bf16[512,256]{1,0:T(8,128)(2,1)} %shard_map.37) | data formatting | bytes 524288

commit v3 on v2

--- a/solution.py
+++ b/solution.py
@@ -8,6 +8,8 @@
 from jax.sharding import PartitionSpec as P
 
 PIECES = 4
+RELAYED = ()
+AHEAD = 2
 PARTS = 2
 MESH = pl.DeviceIdType.MESH
 
@@ -67,8 +69,7 @@
 def kernel(
     n_loop, h_ref, c_ref, t_ref, out_ref,
     slab, tiles, tab_out, tab_in, pools, y_out, sel, cand,
-    same, core_out, core_in, z_out, z_in, z_via, x_out, x_in, direct, d_out, d_in,
-    stack, fin, send, recv, local,
+    same, core_out, core_in, z_out, z_in, direct, d_out, d_in, stack, send, recv, local,
 ):
     half_loop = n_loop // 2
     me = lax.axis_index("loop")
@@ -148,20 +149,12 @@
     for k in range(PIECES):
         cand[k][4] = jnp.zeros(cand[k].shape[1:], bf16)
 
-    @pl.when(z == 0)
-    def _():
-        for k in range(PIECES):
-            z_in[k][0] = jnp.zeros(z_in[k].shape[1:], bf16)
-
-    @pl.when(z == 2)
-    def _():
-        for k in range(PIECES):
-            z_in[k][1] = jnp.zeros(z_in[k].shape[1:], bf16)
-
     barrier = pltpu.get_barrier_semaphore()
-    for peer in (across, core, over_y, at_z(1), at_z(2), at_z(3)):
+    peers = [across, core, over_y]
+    peers += [(at_z(step)[0], lane) for step in (1, 2, 3) for lane in (x, ox)]
+    for peer in peers:
         pl.semaphore_signal(barrier, inc=1, device_id=peer, device_id_type=MESH)
-    pl.semaphore_wait(barrier, 6)
+    pl.semaphore_wait(barrier, len(peers))
 
     piece_in = [
         remote(("piece", k), h_ref.at[other_chunk(k)], pools[k].at[c, :, my_cols], across)
@@ -170,17 +163,22 @@
     table_in = remote(("table",), tab_out, tab_in, across)
 
     z_move, core_move = [], []
-    for k in range(PIECES):
+
+    def send_rows(k):
         own_copies[k].wait()
         piece_in[k].wait_recv()
         one = remote(
-            ("z1", k), pools[k].at[c], pools[k].at[2 + c], at_z(3), when=z != 0
+            ("z1", k), pools[k].at[c], pools[k].at[2 + c], at_z(3),
+            when=z != 0 if k in RELAYED else None,
         )
         two = remote(
-            ("z2", k), pools[k].at[c], pools[k].at[4 + c], at_z(2), when=z != 2
+            ("z2", k), pools[k].at[c], pools[k].at[4 + c], at_z(2),
+            when=z != 2 if k in RELAYED else None,
         )
         z_move.append((one, two))
         core_move.append([remote(("c0", k), pools[k].at[c], pools[k].at[c], core)])
+    for k in range(AHEAD):
+        send_rows(k)
     slab_in = remote(("slab",), h_ref.at[my_rows], slab.at[my_rows, my_cols], across)
 
     def send_tiles(half):
@@ -230,12 +228,12 @@
     def gather_rows(k):
         for step in (1, 2):
             z_move[k][step - 1].wait_recv()
-            if step == 1:
+            if step == 1 and k in RELAYED:
                 remote(
                     ("via1", k), pools[k].at[2 + c], pools[k].at[4 + c], at_z(3),
                     lands=("z2", k), when=z == 1,
                 )
-            else:
+            elif k in RELAYED:
                 remote(
                     ("via2", k), pools[k].at[4 + c], pools[k].at[2 + c], at_z(1),
                     lands=("z1", k), when=z == 2,
@@ -245,6 +243,8 @@
                     ("c", step, k), pools[k].at[2 * step + c], pools[k].at[2 * step + c], core
                 )
             )
+        if k + AHEAD < PIECES:
+            send_rows(k + AHEAD)
         for copy in core_move[k]:
             copy.wait_recv()
         for j in range(2):
@@ -309,66 +309,55 @@
     def send_back(k):
         b_core[k].wait_recv()
 
-        def total(step):
-            return same[k][step] + core_in[k][step].astype(f32)
-
-        for step in (1, 2):
-            z_out[k][step - 1] = total(step).astype(bf16)
-        one, two = z_out[k].at[0], z_out[k].at[1]
-        via = remote(("v0", k), two, z_via[k], at_z(1), lands=("v", k), when=z == 0)
-        remote(("v3", k), one, z_via[k], at_z(3), lands=("v", k), when=z == 3)
-        z_a = remote(
-            ("ba", k), one, z_in[k].at[0], at_z(1), lands=("bz1", k),
-            when=jnp.logical_or(z == 0, z == 2),
-        )
-        z_b = remote(
-            ("bb", k), two, z_in[k].at[1], at_z(2), lands=("bz2", k),
-            when=jnp.logical_or(z == 1, z == 3),
-        )
-
-        @pl.when(z == 1)
-        def _():
-            via.wait_recv()
-            z_out[k][0] = (total(1) + z_via[k][...].astype(f32)).astype(bf16)
-
-        @pl.when(z == 2)
-        def _():
-            via.wait_recv()
-            z_out[k][1] = (total(2) + z_via[k][...].astype(f32)).astype(bf16)
-
-        remote(("bc1", k), one, z_in[k].at[0], at_z(1), lands=("bz1", k), when=z == 1)
-        remote(("bc2", k), two, z_in[k].at[1], at_z(2), lands=("bz2", k), when=z == 2)
-        b_z.append((z_a, z_b))
+        moves = []
+        for step in (2, 1, 0):
+            z_out[k][step] = (same[k][step] + core_in[k][step].astype(f32)).astype(bf16)
+            there = at_z(step)[0]
+            moves.append(remote(
+                ("far", k, step), z_out[k].at[step, :, other_cols], z_in[k].at[1, step], (there, ox)
+            ))
+            if step > 0:
+                moves.append(remote(
+                    ("near", k, step), z_out[k].at[step, :, my_cols], z_in[k].at[0, step], (there, x)
+                ))
+        b_z.append(moves)
 
     def finish(k):
-        pl.when(z != 0)(b_z[k][0].wait_recv)
-        pl.when(z != 2)(b_z[k][1].wait_recv)
-        fin[k] = (
-            same[k][0] + core_in[k][0].astype(f32)
-            + z_in[k][0].astype(f32) + z_in[k][1].astype(f32)
-        )
-        x_out[k][...] = fin[k, :, other_cols].astype(bf16)
-        last.append(remote(("x", k), x_out[k], x_in[k], across))
-
-    for t in range(PIECES + 4):
-        for lag, step in enumerate((gather_rows, compute, sort_back, send_back, finish)):
-            if 0 <= t - lag < PIECES:
-                step(t - lag)
-        if t + 1 < PARTS:
-            tile_in.append(send_tiles(t + 1))
-
+        for copy in b_z[k]:
+            copy.wait_recv()
+        r = my_chunk(k)
+        out_ref[r, :] = (
+            direct[r, my_cols] + d_in[r, :].astype(f32)
+            + same[k][0, :, my_cols] + core_in[k][0, :, my_cols].astype(f32)
+            + z_in[k][0, 1].astype(f32) + z_in[k][0, 2].astype(f32)
+        ).astype(bf16)
+        r = other_chunk(k)
+        out_ref[r, :] = (
+            direct[r, my_cols] + d_in[r, :].astype(f32) + z_in[k][1, 0].astype(f32)
+            + z_in[k][1, 1].astype(f32) + z_in[k][1, 2].astype(f32)
+        ).astype(bf16)
+
+    gather_rows(0)
+    tile_in.append(send_tiles(1))
+    gather_rows(1)
+    compute(0)
+    gather_rows(2)
+    compute(1)
+    sort_back(0)
+    gather_rows(3)
+    send_back(0)
+    compute(2)
+    sort_back(1)
+    send_back(1)
+    compute(3)
+    sort_back(2)
+    send_back(2)
+    sort_back(3)
+    send_back(3)
     last[0].wait_recv()
     for k in range(PIECES):
-        r = my_chunk(k)
-        out_ref[r, :] = (
-            direct[r, my_cols] + d_in[r, :].astype(f32) + fin[k, :, my_cols]
-        ).astype(bf16)
-    for k in range(PIECES):
-        last[k + 1].wait_recv()
-        r = other_chunk(k)
-        out_ref[r, :] = (
-            direct[r, my_cols] + d_in[r, :].astype(f32) + x_in[k][...].astype(f32)
-        ).astype(bf16)
+        finish(k)
+
     for copy, when in started:
         if when is None:
             copy.wait_send()
@@ -376,7 +365,7 @@
             pl.when(when)(copy.wait_send)
 
 
-COPIES = 3 + 2 * PARTS + 24 * PIECES
+COPIES = 3 + 2 * PARTS + 18 * PIECES
 
 
 def planned_body(n_loop, orbitals, coulomb, table):
@@ -409,16 +398,12 @@
             each((3, chunk, full), f32),
             each((3, chunk, full)),
             each((3, chunk, full)),
-            each((2, chunk, full)),
-            each((2, chunk, full)),
-            each((chunk, full)),
-            each((chunk, width)),
-            each((chunk, width)),
+            each((3, chunk, full)),
+            each((2, 3, chunk, width)),
             pltpu.VMEM((points, full), f32),
             pltpu.VMEM((points, width), bf16),
             pltpu.VMEM((points, width), bf16),
             pltpu.VMEM((4 * chunk, full), bf16),
-            pltpu.VMEM((PIECES, chunk, full), f32),
             pltpu.SemaphoreType.DMA((COPIES,)),
             pltpu.SemaphoreType.DMA((COPIES,)),
             pltpu.SemaphoreType.DMA((PIECES + 1 + 2 * PARTS,)),

time: 65.6 us -> 56.7 us (0.86)
  Pallas kernels: 63.7 us -> 54.9 us
    pallas_call x1, Pallas kernels: 63.7 us -> 54.9 us  [planned_body(): pl.pallas_call(functools.partial(kernel, n_loop), out_shape=jax.ShapeDtyp...]
where the time goes in v3:
time: 56.7 us; the launch traced here: 56.5 us
  Pallas kernels  54.9 us (97%)
  local copies, waits for them, and re-layouts  1.67 us (3%)
    pallas_call x1, Pallas kernels, planned_body(): pl.pallas_call(functools.partial(kernel, n_loop), out_shape=jax.ShapeDtyp...  54.9 us
    unnamed x1, local copies, waits for them, and re-layouts  1.67 us

profile of v3, /device:TPU:0, one launch (start us, length us, event | category | flops | bytes accessed | tf_op | source)
XLA Modules:
  0.0 56.5 jit_solution(10727351801070995977)
XLA Ops:
  0.0 54.9 %shard_map.37 = bf16[512,256]{1,0:T(8,128)(2,1)} custom-call(bf16[512,256]{1,0:T(8,128)(2,1)} %h_ref.1, bf16[1,1,2,512,512]{4,3,2,1,0:T(8,128)(2,1)} %c_ref.1, s32[1,2]{1,0:T(1,128)} %t_ref.1), custom_call_target="tpu_custom_call" | custom-call | tf_op jit(solution)/shard_map/pallas_call | solution.py:380
  54.9 1.7 %copy.5 = bf16[512,256]{1,0:T(8,128)(2,1)} copy(bf16[512,256]{1,0:T(8,128)(2,1)} %shard_map.37) | data formatting | bytes 524288
